TPU v7x, 32 devices: a whole 2x2x4 slice. The times are simulated.
32 devices in a mesh: dp: 8 (over z, x), tensor: 4 (over y, core).
Axes of the slice: x: 2, y: 2, z: 4, core: 2. Of those that a mesh axis runs over, the one named last changes fastest.
Arguments:
- hidden_in: bfloat16 [8192, 1024], P(('dp', 'tensor')), may hold values from -6 to 6
- out_grad: bfloat16 [8192, 1024], P(('dp', 'tensor')), may hold values from -6 to 6
- seq_lengths: int32 [8], P('dp'), may hold values from 256 to 1024, as said below
- norm1_gain: float32 [1024], replicated, may hold values from 0.5 to 1.5
- zx_weight: bfloat16 [1024, 2, 1536], P(None, None, 'tensor'), may hold values from -0.1875 to 0.1875
- bc_weight: bfloat16 [1024, 256], replicated, may hold values from -0.1875 to 0.1875
- dt_weight: bfloat16 [1024, 24], P(None, 'tensor'), may hold values from -0.1875 to 0.1875
- convx_weight: float32 [4, 1536], P(None, 'tensor'), may hold values from -3 to 3
- convx_bias: float32 [1536], P('tensor'), may hold values from -0.5 to 0.5
- convbc_weight: float32 [4, 256], replicated, may hold values from -3 to 3
- convbc_bias: float32 [256], replicated, may hold values from -0.5 to 0.5
- dt_bias: float32 [24], P('tensor'), may hold values from -6 to -2.5
- a_log: float32 [24], P('tensor'), may hold values from 0 to 2.77
- d_skip: float32 [24], P('tensor'), may hold values from 0.5 to 1.5
- mnorm_gain: float32 [1536], P('tensor'), may hold values from 0.5 to 1.5
- mo_weight: bfloat16 [1536, 1024], P('tensor'), may hold values from -0.15625 to 0.15625
- q_weight: bfloat16 [1024, 512], P(None, 'tensor'), may hold values from -0.1875 to 0.1875
- kv_weight: bfloat16 [1024, 2, 128], replicated, may hold values from -0.1875 to 0.1875
- o_weight: bfloat16 [512, 1024], P('tensor'), may hold values from -6 to 6
- norm2_gain: float32 [1024], replicated, may hold values from 0.5 to 1.5
- gu_weight: bfloat16 [1024, 2, 2048], P(None, None, 'tensor'), may hold values from -0.1875 to 0.1875
- down_weight: bfloat16 [2048, 1024], P('tensor'), may hold values from -0.125 to 0.125
Outputs:
- hidden_out: float32 [8192, 1024], P(('dp', 'tensor'))
- hidden_grad: float32 [8192, 1024], P(('dp', 'tensor'))
- grad_norm1_gain: float32 [1024], replicated
- grad_zx_weight: float32 [1024, 2, 1536], P(None, None, 'tensor')
- grad_bc_weight: float32 [1024, 256], replicated
- grad_dt_weight: float32 [1024, 24], P(None, 'tensor')
- grad_convx_weight: float32 [4, 1536], P(None, 'tensor')
- grad_convx_bias: float32 [1536], P('tensor')
- grad_convbc_weight: float32 [4, 256], replicated
- grad_convbc_bias: float32 [256], replicated
- grad_dt_bias: float32 [24], P('tensor')
- grad_a_log: float32 [24], P('tensor')
- grad_d_skip: float32 [24], P('tensor')
- grad_mnorm_gain: float32 [1536], P('tensor')
- grad_mo_weight: float32 [1536, 1024], P('tensor')
- grad_q_weight: float32 [1024, 512], P(None, 'tensor')
- grad_kv_weight: float32 [1024, 2, 128], replicated
- grad_o_weight: float32 [512, 1024], P('tensor')
- grad_norm2_gain: float32 [1024], replicated
- grad_gu_weight: float32 [1024, 2, 2048], P(None, None, 'tensor')
- grad_down_weight: float32 [2048, 1024], P('tensor')
Inputs may be any that keep to these rules, and one draw needn't show every extreme that they name: Each sequence's live rows are the first seq_lengths rows of its slot of 1024 rows; some sequence is 1024 long in every draw.
All inputs are finite; a program needn't handle non-finite values.
Results may differ from a plain program's by a relative error of at most 0.02.
Values may be sent and summed in bfloat16 or wider, within the bound.
A program may use at most 128 MiB of HBM per device.

v0:
```python
import jax
import jax.numpy as jnp
from jax import lax
from jax.sharding import PartitionSpec as P

HD = 64
DI = 1536


epsilon = 1e-05


def round_value(value):
    return lax.optimization_barrier(value.astype(jnp.bfloat16)).astype(jnp.float32)


def round_keep(value):
    return (round_value(value), None)


def round_pass(kept, grad):
    return (grad,)


def plain_value(value):
    return value


def plain_keep(value):
    return (value, None)


def plain_round(kept, grad):
    return (round_value(grad),)


def low(value):
    rounder = jax.custom_vjp(round_value)
    rounder.defvjp(round_keep, round_pass)
    return rounder(value)


def low_back(value):
    rounder = jax.custom_vjp(plain_value)
    rounder.defvjp(plain_keep, plain_round)
    return rounder(value)


def matmul(left, right):
    return jnp.dot(left, right)


def contract_heads(form, left, right):
    return jnp.einsum(form, left, right)


def rms_scale(row_block, gain_vector):
    return (
        row_block
        * lax.rsqrt(jnp.mean(row_block * row_block, axis=-1, keepdims=True) + epsilon)
        * gain_vector
    )


def causal_conv(values, kernel, shift_bias):
    tap_count = kernel.shape[0]
    row_count = values.shape[0]
    padded = jnp.pad(values, ((tap_count - 1, 0), (0, 0)))
    summed = jnp.zeros_like(values) + shift_bias
    for offset in range(tap_count):
        summed = summed + kernel[offset] * padded[offset : offset + row_count]
    return summed


def rotate(values, head_count, head_dimension):
    row_count = values.shape[0]
    half_size = head_dimension // 2
    frequency = 10000.0 ** (-2.0 * jnp.arange(half_size, dtype=jnp.float32) / head_dimension)
    angles = jnp.arange(row_count, dtype=jnp.float32)[:, None] * frequency[None, :]
    cosine = jnp.cos(angles)[:, None, :]
    sine_part = jnp.sin(angles)[:, None, :]
    by_head = values.reshape(row_count, head_count, head_dimension)
    front_half = by_head[..., :half_size]
    back_half = by_head[..., half_size:]
    turned = jnp.concatenate(
        [front_half * cosine - back_half * sine_part, back_half * cosine + front_half * sine_part],
        axis=-1,
    )
    return turned.reshape(row_count, head_count * head_dimension)


def mamba_front(
    seq_rows,
    zx_weight,
    bc_weight,
    dt_weight,
    convx_weight,
    convx_bias,
    convbc_weight,
    convbc_bias,
    dt_bias,
    a_log,
    d_skip,
):
    row_count, model_width = seq_rows.shape
    inner_width = convx_weight.shape[1]
    head_count = dt_weight.shape[1]
    head_dimension = inner_width // head_count
    state_size = bc_weight.shape[1] // 2
    projected = low_back(matmul(seq_rows, zx_weight.reshape(model_width, 2 * inner_width)))
    gate_in = projected[:, :inner_width]
    signal = projected[:, inner_width:]
    states_in = low_back(matmul(seq_rows, bc_weight))
    step_raw = low_back(matmul(seq_rows, dt_weight))
    conv_signal = jax.nn.silu(causal_conv(signal, convx_weight, convx_bias))
    conv_states = jax.nn.silu(causal_conv(states_in, convbc_weight, convbc_bias))
    input_map = low(conv_states[:, :state_size])
    output_map = low(conv_states[:, state_size:])
    step_size = jax.nn.softplus(step_raw + dt_bias)
    log_decay = jnp.cumsum(step_size * -jnp.exp(a_log), axis=0)
    state_match = low_back(matmul(output_map, input_map.T))
    position = jnp.arange(row_count)
    causal = position[:, None] >= position[None, :]
    spread = log_decay.T[:, :, None] - log_decay.T[:, None, :]
    decay_matrix = jnp.where(causal[None], jnp.exp(jnp.where(causal[None], spread, 0.0)), 0.0)
    mixing = low(state_match[None] * decay_matrix)
    per_head = conv_signal.reshape(row_count, head_count, head_dimension)
    driven = low(per_head * step_size[:, :, None])
    scanned = low_back(contract_heads("hts,shp->thp", mixing, driven))
    joined = scanned + d_skip[None, :, None] * per_head
    gated_out = joined.reshape(row_count, inner_width) * jax.nn.silu(gate_in)
    return (gated_out, jnp.sum(gated_out * gated_out, axis=1))


def mamba_back(gated_out, square_total, norm_gain, out_weight, full_width):
    normed = low(gated_out * lax.rsqrt(square_total[:, None] / full_width + epsilon) * norm_gain)
    return matmul(normed, out_weight)


def attention_part(
    seq_rows, length, q_weight, kv_weight, o_weight, query_heads, key_heads, head_dimension
):
    row_count, model_width = seq_rows.shape
    queries_raw = low_back(matmul(seq_rows, q_weight))
    key_value = low_back(matmul(seq_rows, kv_weight.reshape(model_width, -1)))
    key_width = key_value.shape[1] // 2
    key_rows = low(rotate(key_value[:, :key_width], key_heads, head_dimension))
    value_rows = low(key_value[:, key_width:])
    queries = low(rotate(queries_raw, query_heads, head_dimension))
    group_size = query_heads // key_heads
    query_tensor = queries.reshape(row_count, key_heads, group_size, head_dimension)
    key_tensor = key_rows.reshape(row_count, key_heads, head_dimension)
    value_tensor = value_rows.reshape(row_count, key_heads, head_dimension)
    attention_scores = low_back(
        contract_heads("ievb,meb->evim", query_tensor, key_tensor) * head_dimension ** (-0.5)
    )
    position = jnp.arange(row_count).astype(jnp.int32)
    allowed = (position[None, :] <= position[:, None]) & (position[None, :] < length)
    masked = jnp.where(allowed, attention_scores, -1e30)
    largest = jnp.max(masked, axis=-1, keepdims=True)
    raised = jnp.exp(masked - largest)
    attention_weights = low(raised / jnp.sum(raised, axis=-1, keepdims=True))
    attended_values = contract_heads("wbql,lwc->qwbc", attention_weights, value_tensor)
    attended_values = low_back(
        low(attended_values.reshape(row_count, query_heads * head_dimension))
    )
    return matmul(attended_values, o_weight)


def ffn_part(seq_rows, gu_weight, down_weight):
    model_width = seq_rows.shape[1]
    projected = low_back(matmul(seq_rows, gu_weight.reshape(model_width, -1)))
    hidden_width = projected.shape[1] // 2
    active = low(jax.nn.silu(projected[:, :hidden_width]) * projected[:, hidden_width:])
    return matmul(active, down_weight)


def shards(
    hidden_in,
    out_grad,
    seq_lengths,
    norm1_gain,
    zx_weight,
    bc_weight,
    dt_weight,
    convx_weight,
    convx_bias,
    convbc_weight,
    convbc_bias,
    dt_bias,
    a_log,
    d_skip,
    mnorm_gain,
    mo_weight,
    q_weight,
    kv_weight,
    o_weight,
    norm2_gain,
    gu_weight,
    down_weight,
):
    model_width = hidden_in.shape[1]
    seq_count = seq_lengths.shape[0]
    tensor_rank = lax.axis_index("tensor")
    tensor_count = lax.axis_size("tensor")
    local_heads = q_weight.shape[1] // HD
    key_heads = kv_weight.shape[2] // HD
    heads_per_key = local_heads * tensor_count // key_heads
    key_index = tensor_rank * local_heads // heads_per_key
    key_start = key_index * HD
    kv_local = lax.dynamic_slice_in_dim(kv_weight, key_start, HD, 2)
    residual = hidden_in.astype(jnp.float32)
    normed_one, norm_one_pull = jax.vjp(rms_scale, residual, norm1_gain)
    gathered_one = lax.all_gather(normed_one.astype(jnp.bfloat16), "tensor", axis=0, tiled=True)
    gathered_one = gathered_one.astype(jnp.float32).reshape(seq_count, -1, model_width)
    slot_length = gathered_one.shape[1]
    position = jnp.arange(slot_length)
    row_mask = (position[None, :] < seq_lengths[:, None]).astype(jnp.float32)
    front_params = (
        zx_weight.astype(jnp.float32),
        bc_weight.astype(jnp.float32),
        dt_weight.astype(jnp.float32),
        convx_weight,
        convx_bias,
        convbc_weight,
        convbc_bias,
        dt_bias,
        a_log,
        d_skip,
    )

    def front_all(seq_block, params):

        def front_one(one_rows):
            return mamba_front(one_rows, *params)

        return lax.map(jax.checkpoint(front_one), seq_block)

    (gated_out, squares), front_pull = jax.vjp(front_all, gathered_one, front_params)
    square_total = lax.psum(squares, "tensor")
    rest_params = (
        mnorm_gain,
        mo_weight.astype(jnp.float32),
        q_weight.astype(jnp.float32),
        kv_local.astype(jnp.float32),
        o_weight.astype(jnp.float32),
    )

    def rest_all(gated_in, totals, seq_block, params):

        def rest_one(seq_item):
            gated_seq, total_seq, rows_seq, length, mask_seq = seq_item
            mamba_out = mamba_back(gated_seq, total_seq, params[0], params[1], DI)
            attn_out = attention_part(
                rows_seq, length, params[2], params[3], params[4], local_heads, 1, HD
            )
            return (mamba_out + attn_out) * mask_seq[:, None]

        return lax.map(
            jax.checkpoint(rest_one), (gated_in, totals, seq_block, seq_lengths, row_mask)
        )

    partial_mix, rest_pull = jax.vjp(rest_all, gated_out, square_total, gathered_one, rest_params)
    mixed_rows = lax.psum_scatter(
        partial_mix.reshape(-1, model_width).astype(jnp.bfloat16),
        "tensor",
        scatter_dimension=0,
        tiled=True,
    ).astype(jnp.float32)
    middle = residual + mixed_rows
    normed_two, norm_two_pull = jax.vjp(rms_scale, middle, norm2_gain)
    gathered_two = lax.all_gather(normed_two.astype(jnp.bfloat16), "tensor", axis=0, tiled=True)
    gathered_two = gathered_two.astype(jnp.float32).reshape(seq_count, -1, model_width)
    ffn_params = (gu_weight.astype(jnp.float32), down_weight.astype(jnp.float32))

    def ffn_all(seq_block, params):

        def ffn_one(seq_item):
            rows_seq, mask_seq = seq_item
            return ffn_part(rows_seq, params[0], params[1]) * mask_seq[:, None]

        return lax.map(jax.checkpoint(ffn_one), (seq_block, row_mask))

    partial_ffn, ffn_pull = jax.vjp(ffn_all, gathered_two, ffn_params)
    ffn_rows = lax.psum_scatter(
        partial_ffn.reshape(-1, model_width).astype(jnp.bfloat16),
        "tensor",
        scatter_dimension=0,
        tiled=True,
    ).astype(jnp.float32)
    hidden_out = middle + ffn_rows
    cotangent = out_grad.astype(jnp.float32)
    ffn_cot = lax.all_gather(cotangent.astype(jnp.bfloat16), "tensor", axis=0, tiled=True)
    ffn_cot = ffn_cot.astype(jnp.float32).reshape(seq_count, -1, model_width)
    d_two_rows, d_ffn_params = ffn_pull(ffn_cot)
    d_two = lax.psum_scatter(
        d_two_rows.reshape(-1, model_width).astype(jnp.bfloat16),
        "tensor",
        scatter_dimension=0,
        tiled=True,
    ).astype(jnp.float32)
    d_middle_part, d_gain_two = norm_two_pull(d_two)
    d_middle = cotangent + d_middle_part
    mixer_cot = lax.all_gather(d_middle.astype(jnp.bfloat16), "tensor", axis=0, tiled=True)
    mixer_cot = mixer_cot.astype(jnp.float32).reshape(seq_count, -1, model_width)
    d_gated, d_totals, d_rows_rest, d_rest = rest_pull(mixer_cot)
    d_squares = lax.psum(d_totals, "tensor")
    d_rows_front, d_front = front_pull((d_gated, d_squares))
    d_one = lax.psum_scatter(
        (d_rows_front + d_rows_rest).reshape(-1, model_width).astype(jnp.bfloat16),
        "tensor",
        scatter_dimension=0,
        tiled=True,
    ).astype(jnp.float32)
    d_resid_part, d_gain_one = norm_one_pull(d_one)
    hidden_grad = d_middle + d_resid_part
    kv_grad = lax.dynamic_update_slice_in_dim(
        jnp.zeros(kv_weight.shape, jnp.float32), d_rest[3], key_start, 2
    )
    shared = lax.psum(
        (d_gain_one, d_front[1], d_front[5], d_front[6], kv_grad, d_gain_two), ("dp", "tensor")
    )
    summed = lax.psum(
        (
            d_front[0],
            d_front[2],
            d_front[3],
            d_front[4],
            d_front[7],
            d_front[8],
            d_front[9],
            d_rest[0],
            d_rest[1],
            d_rest[2],
            d_rest[4],
            d_ffn_params[0],
            d_ffn_params[1],
        ),
        "dp",
    )
    split_grads = summed[:11]
    gu_grad = summed[11]
    down_grad = summed[12]
    return (
        hidden_out,
        hidden_grad,
        shared[0],
        split_grads[0],
        shared[1],
        split_grads[1],
        split_grads[2],
        split_grads[3],
        shared[2],
        shared[3],
        split_grads[4],
        split_grads[5],
        split_grads[6],
        split_grads[7],
        split_grads[8],
        split_grads[9],
        shared[4],
        split_grads[10],
        shared[5],
        gu_grad,
        down_grad,
    )


def solution(mesh):
    return jax.shard_map(
        shards,
        mesh=mesh,
        in_specs=(
            P(("dp", "tensor"), None),
            P(("dp", "tensor"), None),
            P("dp"),
            P(),
            P(None, None, "tensor"),
            P(),
            P(None, "tensor"),
            P(None, "tensor"),
            P("tensor"),
            P(),
            P(),
            P("tensor"),
            P("tensor"),
            P("tensor"),
            P("tensor"),
            P("tensor", None),
            P(None, "tensor"),
            P(),
            P("tensor", None),
            P(),
            P(None, None, "tensor"),
            P("tensor", None),
        ),
        out_specs=(
            P(("dp", "tensor"), None),
            P(("dp", "tensor"), None),
            P(),
            P(None, None, "tensor"),
            P(),
            P(None, "tensor"),
            P(None, "tensor"),
            P("tensor"),
            P(),
            P(),
            P("tensor"),
            P("tensor"),
            P("tensor"),
            P("tensor"),
            P("tensor", None),
            P(None, "tensor"),
            P(),
            P("tensor", None),
            P(),
            P(None, None, "tensor"),
            P("tensor", None),
        ),
        check_vma=False,
    )
```

profile of v0, /device:TPU:0, one launch (start us, length us, event | category | flops | bytes accessed | tf_op | source)
XLA Modules:
  0.0 1170.8 jit_solution(17496257054004414393)
XLA Ops:
  23.7 13.5 %all-gather.5.cloned.1.call-done = bf16[1024,1024]{1,0:T(8,128)(2,1)} async-done(((bf16[256,1024]{1,0:T(8,128)(2,1)}), bf16[1024,1024]{1,0:T(8,128)(2,1)}) %all-gather.5.cloned.1.call-update) | async-done | bytes 2097168 | tf_op jit(solution)/shard_map/all_gather | solution.py:214
  63.3 8.9 multiply_convert_fusion.1
  76.8 8.5 bitcast_add_fusion.1
  87.6 6.6 psum.147
  101.1 31.9 %reduce-scatter.5.cloned.1.call-done = bf16[256,1024]{1,0:T(8,128)(2,1)} async-done(((bf16[1024,1024]{1,0:T(8,128)(2,1)}), bf16[256,1024]{1,0:T(8,128)(2,1)}) %reduce-scatter.5.cloned.1.call-update) | async-done | bytes 524304 | tf_op jit(solution)/shard_map/reduce_scatter | solution.py:264
  138.0 19.3 %all-gather.9.cloned.1.call-done = bf16[1024,1024]{1,0:T(8,128)(2,1)} async-done(((bf16[256,1024]{1,0:T(8,128)(2,1)}), bf16[1024,1024]{1,0:T(8,128)(2,1)}) %all-gather.9.cloned.1.call-update) | async-done | bytes 2097168 | tf_op jit(solution)/shard_map/all_gather | solution.py:293
  161.4 20.6 %all-gather.7.cloned.1.call-done = bf16[1024,1024]{1,0:T(8,128)(2,1)} async-done(((bf16[256,1024]{1,0:T(8,128)(2,1)}), bf16[1024,1024]{1,0:T(8,128)(2,1)}) %all-gather.7.cloned.1.call-update) | async-done | bytes 2097168 | tf_op jit(solution)/shard_map/all_gather | solution.py:272
  195.3 31.5 %reduce-scatter.9.cloned.1.call-done = bf16[256,1024]{1,0:T(8,128)(2,1)} async-done(((bf16[1024,1024]{1,0:T(8,128)(2,1)}), bf16[256,1024]{1,0:T(8,128)(2,1)}) %reduce-scatter.9.cloned.1.call-update) | async-done | bytes 524304 | tf_op jit(solution)/shard_map/reduce_scatter | solution.py:296
  234.7 21.4 %all-gather.11.cloned.1.call-done = bf16[1024,1024]{1,0:T(8,128)(2,1)} async-done(((bf16[256,1024]{1,0:T(8,128)(2,1)}), bf16[1024,1024]{1,0:T(8,128)(2,1)}) %all-gather.11.cloned.1.call-update) | async-done | bytes 2097168 | tf_op jit(solution)/shard_map/all_gather | solution.py:304
  262.3 6.8 psum.148
  286.6 8.4 multiply_convert_fusion
  301.7 8.8 bitcast_add_fusion
  317.0 16.8 %fusion.2 = (f32[6,1024]{1,0:T(8,128)}, f32[6,1024]{1,0:T(8,128)}, bf16[1024,1024]{1,0:T(8,128)(2,1)S(1)}) fusion(f32[6,1024]{1,0:T(8,128)S(1)} %bitcast.413, f32[1024,1024]{1,0:T(8,128)S(1)} %fusion.159, pred[1024,1024]{1,0:T(8,128)(4,1)S(1)} %copy-done.12, bf16[1024,6,64]{0,2,1:T(8,128)(2,1)S(1)} %copy-done.26, ...), kind=kOutput, calls=%fused_computation.7 | convolution fusion | flops 873451520 | bytes 8986624 | tf_op jit(solution)/shard_map/transpose(jvp())/while/body/eval_jaxpr/checkpoint/hts,shp->thp/dot_general | solution.py:54
  361.1 6.8 divide_convert_fusion
  374.7 8.7 reduce-window.44
  387.8 6.4 multiply_reduce_fusion.5
  421.1 7.1 fusion.173
  428.2 7.3 copy.80
  445.4 31.7 %dynamic_update_slice.24 = f32[1024,2,128]{2,1,0:T(2,128)} dynamic-update-slice(f32[1024,2,128]{2,1,0:T(2,128)} %broadcast_in_dim.281, f32[1024,2,64]{2,1,0:T(2,128)} %copy.78, s32[]{:T(128)} %constant.237.clone.1, s32[]{:T(128)} %constant.237.clone.1, s32[]{:T(128)S(6)} %select_n.105) | dynamic-update-slice | bytes 1048580 | tf_op jit(solution)/shard_map/dynamic_update_slice | solution.py:317
  489.4 5.8 copy.76
  502.6 38.3 %all-reduce.34 = (f32[1024,6]{0,1:T(8,128)}, f32[4,384]{1,0:T(4,128)}, f32[384]{0:T(512)}, f32[6]{0:T(128)}, f32[6]{0:T(128)}, /*index=5*/f32[6]{0:T(128)}, f32[384]{0:T(512)}) all-reduce(f32[1024,6]{0,1:T(8,128)S(1)} %fusion.170, f32[4,384]{1,0:T(4,128)S(1)} %pad_add_fusion.6, ...), channel_id=1, replica_groups=mesh['dp'=8,'tensor'=4] {'dp'}, use_global_device_ids=true, to_apply=%region_33.34 | all-reduce | flops 8466 | bytes 67728 | tf_op jit(solution)/shard_map/psum | solution.py:323
  542.6 174.6 %all-reduce.32 = (f32[1024]{0:T(1024)}, f32[4,256]{1,0:T(4,128)}, f32[256]{0:T(256)}, f32[1024]{0:T(1024)}) all-reduce(f32[1024]{0:T(1024)S(1)} %get-tuple-element.675, f32[4,256]{1,0:T(4,128)S(1)} %pad_add_fusion.7, f32[256]{0:T(256)S(1)} %copy-done.140, f32[1024]{0:T(1024)S(1)} %copy-done.100), channel_id=1, replica_groups=mesh['dp'=8,'tensor'=4] {'dp','tensor'}, use_global_device_ids=true, to_apply=%region_30.31 | all-reduce | flops 3328 | bytes 26624 | tf_op jit(solution)/shard_map/psum | solution.py:320
  721.3 36.6 %all-reduce.39.cloned.1.call-done = (f32[1024,256]{1,0:T(8,128)}, f32[1024,2,128]{2,1,0:T(2,128)}) async-done(((f32[1024,256]{1,0:T(8,128)}, f32[1024,2,128]{2,1,0:T(2,128)}), (f32[1024,256]{1,0:T(8,128)}, f32[1024,2,128]{2,1,0:T(2,128)})) %all-reduce.39.cloned.1.call-update) | async-done | bytes 2097168 | tf_op jit(solution)/shard_map/psum | solution.py:320
  757.8 390.8 %all-reduce.41.cloned.1.call-done = (f32[1024,2,384]{2,1,0:T(2,128)}, f32[384,1024]{1,0:T(8,128)}, f32[1024,128]{1,0:T(8,128)}, f32[128,1024]{1,0:T(8,128)}, f32...) async-done(((f32[1024,2,384]{2,1,0:T(2,128)}, f32[384,1024]{1,0:T(8,128)}, f32[1024,128]{1,0:T(8,128)}, f32[128,1024]{1,0:T(8,128)}, f32[1024,2,512]{2,1,0:T(2,128)}, ...) | async-done | bytes 12058640 | tf_op jit(solution)/shard_map/psum | solution.py:323
  (513 shorter events, 236.8 us)
Async XLA Ops:
  7.2 179.5 %copy-start = (bf16[512,1024]{1,0:T(8,128)(2,1)S(1)}, bf16[512,1024]{1,0:T(8,128)(2,1)}, u32[]{:S(2)}) copy-start(bf16[512,1024]{1,0:T(8,128)(2,1)} %param.43) | copy-start | bytes 3145732
  7.2 30.0 %all-gather.5.cloned.1.call-start = ((), (), s32[]{:S(2)}) async-start(), calls=%async_computation.4 | async-start | bytes 2621440 | tf_op jit(solution)/shard_map/all_gather | solution.py:214
  11.8 121.3 %reduce-scatter.5.cloned.1.call-start = ((), (), s32[]{:S(2)}) async-start(), calls=%async_computation.5 | async-start | bytes 2621440 | tf_op jit(solution)/shard_map/reduce_scatter | solution.py:264
  17.6 22.3 %copy-start.118 = (f32[32]{0:T(128)}, f32[32]{0:T(128)S(1)}, u32[]{:S(2)}) copy-start(f32[32]{0:T(128)S(1)} %multiply_power_fusion) | copy-start | bytes 388
  100.4 56.9 %all-gather.9.cloned.1.call-start = ((), (), s32[]{:S(2)}) async-start(), calls=%async_computation.8 | async-start | bytes 2621440 | tf_op jit(solution)/shard_map/all_gather | solution.py:293
  101.1 80.9 %all-gather.7.cloned.1.call-start = ((), (), s32[]{:S(2)}) async-start(), calls=%async_computation.6 | async-start | bytes 2621440 | tf_op jit(solution)/shard_map/all_gather | solution.py:272
  137.8 89.1 %reduce-scatter.9.cloned.1.call-start = ((), (), s32[]{:S(2)}) async-start(), calls=%async_computation.9 | async-start | bytes 2621440 | tf_op jit(solution)/shard_map/reduce_scatter | solution.py:296
  195.3 60.7 %all-gather.11.cloned.1.call-start = ((), (), s32[]{:S(2)}) async-start(), calls=%async_computation.10 | async-start | bytes 2621440 | tf_op jit(solution)/shard_map/all_gather | solution.py:304
  233.3 307.6 %reduce-scatter.11.cloned.1.call-start = ((), (), s32[]{:S(2)}) async-start(), calls=%async_computation.11 | async-start | bytes 2621440 | tf_op jit(solution)/shard_map/reduce_scatter | solution.py:309
  413.0 304.3 %reduce-scatter.7.cloned.1.call-start = ((), (), s32[]{:S(2)}) async-start(), calls=%async_computation.7 | async-start | bytes 2621440 | tf_op jit(solution)/shard_map/reduce_scatter | solution.py:285
  421.1 336.8 %all-reduce.39.cloned.1.call-start = ((), (), s32[]{:S(2)}) async-start(), calls=%async_computation.12 | async-start | bytes 4194304 | tf_op jit(solution)/shard_map/psum | solution.py:320
  484.8 663.9 %all-reduce.41.cloned.1.call-start = ((), (), s32[]{:S(2)}) async-start(), calls=%async_computation.13 | async-start | bytes 24117248 | tf_op jit(solution)/shard_map/psum | solution.py:323
  501.3 39.6 %copy-start.141 = (f32[256]{0:T(256)S(1)}, f32[256]{0:T(256)}, u32[]{:S(2)}) copy-start(f32[256]{0:T(256)} %get-tuple-element.666) | copy-start | bytes 3076
  501.3 39.5 %copy-start.142 = (f32[256]{0:T(256)S(1)}, f32[256]{0:T(256)}, u32[]{:S(2)}) copy-start(f32[256]{0:T(256)} %get-tuple-element.667) | copy-start | bytes 3076
  501.3 39.5 %copy-start.143 = (f32[256]{0:T(256)S(1)}, f32[256]{0:T(256)}, u32[]{:S(2)}) copy-start(f32[256]{0:T(256)} %get-tuple-element.668) | copy-start | bytes 3076
  501.3 39.5 %copy-start.144 = (f32[256]{0:T(256)S(1)}, f32[256]{0:T(256)}, u32[]{:S(2)}) copy-start(f32[256]{0:T(256)} %get-tuple-element.669) | copy-start | bytes 3076
  501.3 39.6 %copy-start.83 = (f32[1024]{0:T(1024)S(1)}, f32[1024]{0:T(1024)}, u32[]{:S(2)}) copy-start(f32[1024]{0:T(1024)} %param.25) | copy-start | bytes 12292
  501.4 39.6 %copy-start.104 = (f32[256]{0:T(256)S(1)}, f32[256]{0:T(256)}, u32[]{:S(2)}) copy-start(f32[256]{0:T(256)} %copy-done.103) | copy-start | bytes 3076
  501.4 41.3 %copy-start.100 = (f32[1024]{0:T(1024)S(1)}, f32[1024]{0:T(1024)}, u32[]{:S(2)}) copy-start(f32[1024]{0:T(1024)} %get-tuple-element.670) | copy-start | bytes 12292
  501.4 41.2 %copy-start.140 = (f32[256]{0:T(256)S(1)}, f32[256]{0:T(256)}, u32[]{:S(2)}) copy-start(f32[256]{0:T(256)} %get-tuple-element.674) | copy-start | bytes 3076
  501.4 215.9 %copy-start.116 = (f32[256]{0:T(256)S(1)}, f32[256]{0:T(256)}, u32[]{:S(2)}) copy-start(f32[256]{0:T(256)} %copy-done.115) | copy-start | bytes 3076
  501.4 215.9 %copy-start.82 = (f32[1024]{0:T(1024)S(1)}, f32[1024]{0:T(1024)}, u32[]{:S(2)}) copy-start(f32[1024]{0:T(1024)} %param.41) | copy-start | bytes 12292
  501.4 215.9 %copy-start.87 = (f32[256]{0:T(256)S(1)}, f32[256]{0:T(256)}, u32[]{:S(2)}) copy-start(f32[256]{0:T(256)} %copy-done.86) | copy-start | bytes 3076
  501.4 215.9 %copy-start.106 = (f32[256]{0:T(256)S(1)}, f32[256]{0:T(256)}, u32[]{:S(2)}) copy-start(f32[256]{0:T(256)} %copy-done.105) | copy-start | bytes 3076
  (146 other events, 440.1 us)
Sparse Core Ops, SparseCore 0:
  11.9 25.2 all-gather.4
  100.5 32.5 reduce-scatter.4
  134.7 22.5 all-gather.8
  159.3 22.5 all-gather.6
  195.4 31.3 reduce-scatter.8
  233.4 22.5 all-gather.10
  413.1 32.4 reduce-scatter.10
  448.3 31.5 reduce-scatter.6
  486.6 271.1 all-reduce.38
  765.3 383.3 all-reduce.40
where the time goes:
time: 1180 us; the launch traced here: 1170 us
  waiting for transfers between devices  566 us (48%)
  blocking collectives  226 us (19%)
  matrix products  136 us (12%)
  other arithmetic  121 us (10%)
  local copies, waits for them, and re-layouts  104 us (9%)
  between operations  17 us (1%)
    psum x1, waiting for transfers between devices, shards(): lax.psum((d_front[0], d_front[2], d_front[3], d_front[4], d_front[7], d_f...  391 us
    psum x1, blocking collectives, shards(): lax.psum((d_gain_one, d_front[1], d_front[5], d_front[6], kv_grad, d_gain...  175 us
    dot_general x37, matrix products, matmul(): return jnp.dot(left, right)  77.7 us
    dot_general x12, matrix products, contract_heads(): return jnp.einsum(form, left, right)  58.1 us
    unnamed x338, local copies, waits for them, and re-layouts  40.2 us
    psum x1, blocking collectives, shards(): lax.psum((d_front[0], d_front[2], d_front[3], d_front[4], d_front[7], d_f...  38.3 us
    psum x1, waiting for transfers between devices, shards(): lax.psum((d_gain_one, d_front[1], d_front[5], d_front[6], kv_grad, d_gain...  36.6 us
    reduce_scatter x1, waiting for transfers between devices, shards(): lax.psum_scatter(partial_mix.reshape(-1, model_width).astype(jnp.bfloat16...  31.9 us
  transfers between devices with their start and end apart: 10, of which 8 were waited for; matrix products, arithmetic and copies ran while one was open for 10% of the time, Pallas kernels for 0%

commit v1 on v0

v1 whole, which is shorter than its diff:
```python
import jax
import jax.numpy as jnp
from jax import lax
from jax.sharding import PartitionSpec as P

HD = 64
DI = 1536
BLOCK = 256
BF = jnp.bfloat16
F32 = jnp.float32

epsilon = 1e-05


def mm(left, right):
    return lax.dot_general(left, right, (((1,), (0,)), ((), ())), preferred_element_type=F32)


def mm_nt(left, right):
    return lax.dot_general(left, right, (((1,), (1,)), ((), ())), preferred_element_type=F32)


def mm_tn(left, right):
    return lax.dot_general(left, right, (((0,), (0,)), ((), ())), preferred_element_type=F32)


def heads_dot(form, left, right):
    return jnp.einsum(form, left, right, preferred_element_type=F32)


def after(value, *others):
    return lax.optimization_barrier((value,) + others)[0]


def rms_scale(row_block, gain_vector):
    return (
        row_block
        * lax.rsqrt(jnp.mean(row_block * row_block, axis=-1, keepdims=True) + epsilon)
        * gain_vector
    )


def conv_silu(values, kernel, shift_bias):
    tap_count = kernel.shape[0]
    row_count = values.shape[0]
    padded = jnp.pad(values, ((tap_count - 1, 0), (0, 0)))
    summed = jnp.zeros_like(values) + shift_bias
    for offset in range(tap_count):
        summed = summed + kernel[offset] * padded[offset : offset + row_count]
    return jax.nn.silu(summed)


def running_sum(values):
    row_count, width = values.shape
    size = 128 if row_count % 128 == 0 else row_count
    parts = values.reshape(row_count // size, size, width)
    low_tri = jnp.tril(jnp.ones((size, size), F32))
    inside = jnp.einsum("ij,bjh->bih", low_tri, parts, precision=lax.Precision.HIGHEST)
    count = row_count // size
    strict = jnp.tril(jnp.ones((count, count), F32), -1)
    before = jnp.einsum("cb,bh->ch", strict, inside[:, -1, :], precision=lax.Precision.HIGHEST)
    return (inside + before[:, None, :]).reshape(row_count, width)


def steps(step_raw, dt_bias, a_log):
    step_size = jax.nn.softplus(step_raw + dt_bias)
    return step_size, running_sum(step_size * -jnp.exp(a_log))


def gate_heads(scanned, conv_signal, gate_in, d_skip):
    joined = scanned + jnp.repeat(d_skip, HD)[None, :] * conv_signal
    gated_out = joined * jax.nn.silu(gate_in)
    return gated_out, jnp.sum(gated_out * gated_out, axis=1)


def gated_norm(gated_out, square_total, norm_gain):
    return gated_out * lax.rsqrt(square_total[:, None] / DI + epsilon) * norm_gain


def swiglu(gate_rows, up_rows):
    return jax.nn.silu(gate_rows) * up_rows


def rotate(values, cosine, sine_part):
    row_count, width = values.shape
    half_size = HD // 2
    by_head = values.reshape(row_count, width // HD, HD)
    front_half = by_head[..., :half_size]
    back_half = by_head[..., half_size:]
    turned = jnp.concatenate(
        [front_half * cosine - back_half * sine_part, back_half * cosine + front_half * sine_part],
        axis=-1,
    )
    return turned.reshape(row_count, width)


def split_heads(values):
    return values.reshape(values.shape[0], -1, HD).transpose(1, 0, 2)


def join_heads(values):
    return values.transpose(1, 0, 2).reshape(values.shape[1], -1)


def blocks_of(row_count):
    size = BLOCK if row_count % BLOCK == 0 else row_count
    return [(start, start + size) for start in range(0, row_count, size)]


def stack_blocks(parts, blocks, axis):
    columns = []
    for start, stop in blocks:
        total = None
        for part in parts:
            if part.shape[axis] >= stop:
                piece = lax.slice_in_dim(part, start, stop, axis=axis)
                total = piece if total is None else total + piece
        columns.append(total)
    return jnp.concatenate(columns, axis=axis)


def causal_mask(start, stop):
    return jnp.arange(start, stop)[:, None] >= jnp.arange(stop)[None, :]


def decay_block(decay_heads, start, stop):
    spread = decay_heads[:, start:stop, None] - decay_heads[:, None, :stop]
    return jnp.exp(jnp.where(causal_mask(start, stop)[None], spread, -jnp.inf))


def scan_forward(output_map, input_map, decay_heads, driven):
    blocks = blocks_of(output_map.shape[0])
    mixed, outs = [], []
    for start, stop in blocks:
        match = mm_nt(output_map[start:stop], input_map[:stop])
        mixing = (match[None] * decay_block(decay_heads, start, stop)).astype(BF)
        mixed.append(mixing)
        outs.append(heads_dot("hts,hsp->htp", mixing, driven[:, :stop]))
    return jnp.concatenate(outs, axis=1), mixed


def scan_backward(output_map, input_map, decay_heads, driven, mixed, d_scanned):
    blocks = blocks_of(output_map.shape[0])
    d_driven, d_output, d_input = [], [], []
    for (start, stop), mixing in zip(blocks, mixed):
        cot = d_scanned[:, start:stop]
        d_driven.append(heads_dot("hts,htp->hsp", mixing, cot))
        d_mixing = heads_dot("htp,hsp->hts", cot, driven[:, :stop])
        d_match = jnp.sum(d_mixing * decay_block(decay_heads, start, stop), axis=0).astype(BF)
        d_output.append(mm(d_match, input_map[:stop]))
        d_input.append(mm_tn(d_match, output_map[start:stop]))
    return (
        stack_blocks(d_driven, blocks, 1),
        jnp.concatenate(d_output, axis=0),
        stack_blocks(d_input, blocks, 0),
    )


def attend_forward(queries, keys, values, length):
    blocks = blocks_of(keys.shape[0])
    kept, outs = [], []
    for start, stop in blocks:
        scores = heads_dot("htp,sp->hts", queries[:, start:stop], keys[:stop]) * HD ** (-0.5)
        allowed = causal_mask(start, stop) & (jnp.arange(stop)[None, :] < length)
        masked = jnp.where(allowed[None], scores, -1e30)
        raised = jnp.exp(masked - jnp.max(masked, axis=-1, keepdims=True))
        weights = (raised / jnp.sum(raised, axis=-1, keepdims=True)).astype(BF)
        kept.append(weights)
        outs.append(heads_dot("hts,sp->htp", weights, values[:stop]))
    return jnp.concatenate(outs, axis=1), kept


def attend_backward(queries, keys, values, kept, attended, d_attended):
    blocks = blocks_of(keys.shape[0])
    inner = jnp.sum(attended * d_attended.astype(F32), axis=-1, keepdims=True)
    d_queries, d_keys, d_values = [], [], []
    for (start, stop), weights in zip(blocks, kept):
        cot = d_attended[:, start:stop]
        d_weights = heads_dot("htp,sp->hts", cot, values[:stop])
        d_scores = (weights.astype(F32) * (d_weights - inner[:, start:stop])).astype(BF)
        d_values.append(heads_dot("hts,htp->sp", weights, cot))
        d_queries.append(heads_dot("hts,sp->htp", d_scores, keys[:stop]) * HD ** (-0.5))
        d_keys.append(heads_dot("hts,htp->sp", d_scores, queries[:, start:stop]) * HD ** (-0.5))
    return (
        jnp.concatenate(d_queries, axis=1),
        stack_blocks(d_keys, blocks, 0),
        stack_blocks(d_values, blocks, 0),
    )


def gather_rows(values):
    return lax.all_gather(values.astype(BF), "tensor", axis=0, tiled=True)


def scatter_rows(values):
    return lax.psum_scatter(
        values.astype(BF), "tensor", scatter_dimension=0, tiled=True
    ).astype(F32)


def shards(
    hidden_in,
    out_grad,
    seq_lengths,
    norm1_gain,
    zx_weight,
    bc_weight,
    dt_weight,
    convx_weight,
    convx_bias,
    convbc_weight,
    convbc_bias,
    dt_bias,
    a_log,
    d_skip,
    mnorm_gain,
    mo_weight,
    q_weight,
    kv_weight,
    o_weight,
    norm2_gain,
    gu_weight,
    down_weight,
):
    model_width = hidden_in.shape[1]
    tensor_rank = lax.axis_index("tensor")
    tensor_count = lax.axis_size("tensor")
    inner = zx_weight.shape[2]
    head_count = dt_weight.shape[1]
    q_width = q_weight.shape[1]
    bc_width = bc_weight.shape[1]
    state_size = bc_width // 2
    kv_width = kv_weight.shape[2]
    key_heads = kv_width // HD
    local_heads = q_width // HD
    heads_per_key = local_heads * tensor_count // key_heads
    key_start = (tensor_rank * local_heads // heads_per_key) * HD
    kv_local = lax.dynamic_slice_in_dim(kv_weight, key_start, HD, 2)
    dt_pad = -head_count % 128
    weights_in = jnp.concatenate(
        [
            zx_weight[:, 0],
            zx_weight[:, 1],
            q_weight,
            bc_weight,
            kv_local[:, 0],
            kv_local[:, 1],
            jnp.pad(dt_weight, ((0, 0), (0, dt_pad))),
        ],
        axis=1,
    )
    ends = [inner, 2 * inner, 2 * inner + q_width]
    ends += [ends[2] + bc_width, ends[2] + bc_width + HD, ends[2] + bc_width + 2 * HD]
    gu_flat = jnp.concatenate([gu_weight[:, 0], gu_weight[:, 1]], axis=1)
    ff = gu_weight.shape[2]

    residual = hidden_in.astype(F32)
    normed_one, norm_one_pull = jax.vjp(rms_scale, residual, norm1_gain)
    rows_one = gather_rows(normed_one)
    row_count = rows_one.shape[0]
    length = seq_lengths[0]
    mask = (jnp.arange(row_count) < length)[:, None]
    angles = (
        jnp.arange(row_count, dtype=F32)[:, None]
        * (10000.0 ** (-2.0 * jnp.arange(HD // 2, dtype=F32) / HD))[None, :]
    )
    cosine = jnp.cos(angles)[:, None, :]
    sine_part = jnp.sin(angles)[:, None, :]

    projected = mm(rows_one, weights_in)
    gate_in, signal, q_raw, states_in, key_raw, value_raw, step_pad = jnp.split(
        projected, ends, axis=1
    )
    step_raw = step_pad[:, :head_count]
    conv_signal, signal_pull = jax.vjp(conv_silu, signal, convx_weight, convx_bias)
    conv_states, states_pull = jax.vjp(conv_silu, states_in, convbc_weight, convbc_bias)
    input_map = conv_states[:, :state_size].astype(BF)
    output_map = conv_states[:, state_size:].astype(BF)
    (step_size, log_decay), steps_pull = jax.vjp(steps, step_raw, dt_bias, a_log)
    decay_heads = log_decay.T
    step_wide = jnp.repeat(step_size, HD, axis=1)
    driven_rows = lax.optimization_barrier((conv_signal * step_wide).astype(BF))
    driven = split_heads(driven_rows)
    scanned_heads, mixed = scan_forward(output_map, input_map, decay_heads, driven)
    scanned = join_heads(scanned_heads)
    (gated_out, squares), gate_pull = jax.vjp(gate_heads, scanned, conv_signal, gate_in, d_skip)
    square_total = lax.psum(squares, "tensor")

    queries, rope_q_pull = jax.vjp(lambda v: rotate(v, cosine, sine_part), q_raw)
    key_rows, rope_k_pull = jax.vjp(lambda v: rotate(v, cosine, sine_part), key_raw)
    queries = split_heads(queries.astype(BF))
    key_rows = key_rows.astype(BF)
    value_rows = value_raw.astype(BF)
    attended_heads, kept = attend_forward(queries, key_rows, value_rows, length)
    attended = join_heads(attended_heads).astype(BF)

    normed_gate, gated_pull = jax.vjp(gated_norm, gated_out, square_total, mnorm_gain)
    normed_gate = normed_gate.astype(BF)
    out_parts = jnp.concatenate([normed_gate, attended], axis=1)
    out_weights = jnp.concatenate([mo_weight, o_weight], axis=0)
    partial_mix = jnp.where(mask, mm(out_parts, out_weights), 0.0)
    middle = residual + scatter_rows(partial_mix)
    normed_two, norm_two_pull = jax.vjp(rms_scale, middle, norm2_gain)
    rows_two = gather_rows(normed_two)
    out_cot = jnp.where(mask, gather_rows(out_grad), 0)

    gu_rows = mm(rows_two, gu_flat)
    active, swiglu_pull = jax.vjp(swiglu, gu_rows[:, :ff], gu_rows[:, ff:])
    active = active.astype(BF)
    d_gate_rows, d_up_rows = swiglu_pull(mm_nt(out_cot, down_weight))
    d_gu_rows = jnp.concatenate([d_gate_rows.astype(BF), d_up_rows.astype(BF)], axis=1)
    d_two = scatter_rows(mm_nt(d_gu_rows, gu_flat))
    d_middle_part, d_gain_two = norm_two_pull(d_two)
    d_middle = out_grad.astype(F32) + d_middle_part
    mixer_cot = gather_rows(d_middle)
    partial_ffn = after(jnp.where(mask, mm(active, down_weight), 0.0).astype(BF), mixer_cot)
    hidden_out = middle + scatter_rows(partial_ffn)
    gu_part = after(mm_tn(rows_two, d_gu_rows).astype(BF), mixer_cot)
    down_part = after(mm_tn(active, out_cot).astype(BF), mixer_cot)
    gu_sum, down_sum = lax.psum((gu_part, down_part), "dp")

    mixer_cot = jnp.where(mask, mixer_cot, 0)
    d_out_parts = mm_nt(mixer_cot, out_weights)
    out_part = mm_tn(out_parts, mixer_cot).astype(BF)
    out_sum = lax.psum(after(out_part, gu_sum), "dp")
    d_gated, d_totals, d_mnorm = gated_pull(d_out_parts[:, :inner])
    d_squares = lax.psum(d_totals, "tensor")

    d_attended = split_heads(lax.optimization_barrier(d_out_parts[:, inner:].astype(BF)))
    d_queries, d_keys, d_values = attend_backward(
        queries, key_rows, value_rows, kept, attended_heads, d_attended
    )
    (d_q_raw,) = rope_q_pull(join_heads(d_queries))
    (d_key_raw,) = rope_k_pull(d_keys)

    d_scanned, d_signal_skip, d_gate_in, d_skip_grad = gate_pull((d_gated, d_squares))
    d_scanned = lax.optimization_barrier(d_scanned.astype(BF))
    d_driven_heads, d_output, d_input = scan_backward(
        output_map, input_map, decay_heads, driven, mixed, split_heads(d_scanned)
    )
    d_driven = join_heads(d_driven_heads)
    driven_wide = driven_rows.astype(F32)

    def by_head(values):
        return jnp.sum(values.reshape(row_count, head_count, HD), axis=2)

    d_log_decay = by_head(scanned * d_scanned.astype(F32) - driven_wide * d_driven)
    d_step = by_head(conv_signal * d_driven)
    d_step_raw, d_dt_bias, d_a_log = steps_pull((d_step, d_log_decay))
    d_signal, d_convx, d_convx_bias = signal_pull(d_signal_skip + d_driven * step_wide)
    d_states, d_convbc, d_convbc_bias = states_pull(jnp.concatenate([d_input, d_output], axis=1))

    d_projected = jnp.concatenate(
        [
            d_gate_in.astype(BF),
            d_signal.astype(BF),
            d_q_raw.astype(BF),
            d_states.astype(BF),
            d_key_raw.astype(BF),
            d_values.astype(BF),
            jnp.pad(d_step_raw.astype(BF), ((0, 0), (0, dt_pad))),
        ],
        axis=1,
    )
    d_one = scatter_rows(mm_nt(d_projected, weights_in))
    in_part = mm_tn(rows_one, d_projected)
    kv_part = in_part[:, ends[3] : ends[5]].astype(BF).reshape(model_width, 2, HD)
    kv_placed = lax.dynamic_update_slice_in_dim(
        jnp.zeros(kv_weight.shape, BF), kv_part, key_start, 2
    )
    shared_part = jnp.concatenate(
        [in_part[:, ends[2] : ends[3]].astype(BF), kv_placed[:, 0], kv_placed[:, 1]], axis=1
    )
    split_part = after(in_part[:, : ends[2]].astype(BF), out_sum)
    shared_rows = lax.psum_scatter(shared_part, "tensor", scatter_dimension=0, tiled=True)
    split_sum, shared_rows = lax.psum((split_part, shared_rows), "dp")
    shared_sum = lax.all_gather(shared_rows, "tensor", axis=0, tiled=True).astype(F32)

    d_resid_part, d_gain_one = norm_one_pull(d_one)
    hidden_grad = d_middle + d_resid_part

    own = [
        in_part[:, ends[5] : ends[5] + head_count].T,
        d_convx,
        d_convx_bias,
        d_dt_bias,
        d_a_log,
        d_skip_grad,
        d_mnorm,
    ]
    common = [d_gain_one, d_gain_two, d_convbc, d_convbc_bias]

    def pack(arrays, axes):
        flat = jnp.concatenate([array.reshape(-1) for array in arrays])
        total = lax.psum(flat, axes)
        pieces, start = [], 0
        for array in arrays:
            pieces.append(total[start : start + array.size].reshape(array.shape))
            start += array.size
        return pieces

    dt_sum, convx_sum, convx_bias_sum, dt_bias_sum, a_log_sum, skip_sum, mnorm_sum = pack(
        own, "dp"
    )
    gain_one_sum, gain_two_sum, convbc_sum, convbc_bias_sum = pack(common, ("dp", "tensor"))

    split_sum = split_sum.astype(F32)
    out_sum = out_sum.astype(F32)
    gu_sum = gu_sum.astype(F32)
    return (
        hidden_out,
        hidden_grad,
        gain_one_sum,
        jnp.stack([split_sum[:, :inner], split_sum[:, inner : 2 * inner]], axis=1),
        shared_sum[:, :bc_width],
        dt_sum.T,
        convx_sum,
        convx_bias_sum,
        convbc_sum,
        convbc_bias_sum,
        dt_bias_sum,
        a_log_sum,
        skip_sum,
        mnorm_sum,
        out_sum[:inner],
        split_sum[:, 2 * inner :],
        jnp.stack(
            [shared_sum[:, bc_width : bc_width + kv_width], shared_sum[:, bc_width + kv_width :]],
            axis=1,
        ),
        out_sum[inner:],
        gain_two_sum,
        jnp.stack([gu_sum[:, :ff], gu_sum[:, ff:]], axis=1),
        down_sum.astype(F32),
    )


def solution(mesh):
    return jax.shard_map(
        shards,
        mesh=mesh,
        in_specs=(
            P(("dp", "tensor"), None),
            P(("dp", "tensor"), None),
            P("dp"),
            P(),
            P(None, None, "tensor"),
            P(),
            P(None, "tensor"),
            P(None, "tensor"),
            P("tensor"),
            P(),
            P(),
            P("tensor"),
            P("tensor"),
            P("tensor"),
            P("tensor"),
            P("tensor", None),
            P(None, "tensor"),
            P(),
            P("tensor", None),
            P(),
            P(None, None, "tensor"),
            P("tensor", None),
        ),
        out_specs=(
            P(("dp", "tensor"), None),
            P(("dp", "tensor"), None),
            P(),
            P(None, None, "tensor"),
            P(),
            P(None, "tensor"),
            P(None, "tensor"),
            P("tensor"),
            P(),
            P(),
            P("tensor"),
            P("tensor"),
            P("tensor"),
            P("tensor"),
            P("tensor", None),
            P(None, "tensor"),
            P(),
            P("tensor", None),
            P(),
            P(None, None, "tensor"),
            P("tensor", None),
        ),
        check_vma=False,
    )
```

time: 1180 us -> 787 us (0.67)
  waiting for transfers between devices: 566 us -> 352 us
  blocking collectives: 226 us -> 91.9 us
  other arithmetic: 121 us -> 91.4 us
  matrix products: 136 us -> 124 us
    psum x2 -> x3, waiting for transfers between devices: 427 us -> 174 us  [the longest x1 68.5 us: shards(): split_sum, shared_rows = lax.psum((split_part, shared_rows), 'dp')]
    psum x2, blocking collectives: 213 us -> 79.8 us  [pack(): total = lax.psum(flat, axes)]
    reduce_scatter x4 -> x5, waiting for transfers between devices: 63.4 us -> 126 us  [the longest x4 97.8 us: scatter_rows(): lax.psum_scatter(values.astype(BF), 'tensor', scatter_dimension=0, tiled=...]
    dynamic_update_slice x1, local copies, waits for them, and re-layouts: 31.7 us -> 2.07 us  [shards(): lax.dynamic_update_slice_in_dim(jnp.zeros(kv_weight.shape, BF), kv_part,...]
    all_gather x4 -> x5, waiting for transfers between devices: 74.8 us -> 51.9 us  [the longest x4 51.9 us: gather_rows(): return lax.all_gather(values.astype(BF), 'tensor', axis=0, tiled=True)]
    another operation x13 -> x9, other arithmetic: 26.1 us -> 6.25 us
    dot_general x49 -> x60, matrix products: 136 us -> 116 us  [the longest x32 38.5 us: heads_dot(): return jnp.einsum(form, left, right, preferred_element_type=F32)]
    slice x10 -> x26, local copies, waits for them, and re-layouts: 4.71 us -> 23.5 us  [the longest x1 6.02 us: shards(): gu_flat = jnp.concatenate([gu_weight[:, 0], gu_weight[:, 1]], axis=1)]
  transfers between devices with their start and end apart: 10 -> 13, of which waited for: 8 -> 11; matrix products, arithmetic and copies ran while one was open for 10% -> 20% of each run, Pallas kernels for 0% -> 0%
where the time goes in v1:
time: 787 us; the launch traced here: 782 us
  waiting for transfers between devices  352 us (45%)
  matrix products  124 us (16%)
  local copies, waits for them, and re-layouts  105 us (13%)
  blocking collectives  91.9 us (12%)
  other arithmetic  91.4 us (12%)
  between operations  16.9 us (2%)
    reduce_scatter x4, waiting for transfers between devices, scatter_rows(): lax.psum_scatter(values.astype(BF), 'tensor', scatter_dimension=0, tiled=...  97.8 us
    psum x2, blocking collectives, pack(): total = lax.psum(flat, axes)  79.8 us
    psum x1, waiting for transfers between devices, shards(): split_sum, shared_rows = lax.psum((split_part, shared_rows), 'dp')  68.5 us
    psum x1, waiting for transfers between devices, shards(): out_sum = lax.psum(after(out_part, gu_sum), 'dp')  61.9 us
    all_gather x4, waiting for transfers between devices, gather_rows(): return lax.all_gather(values.astype(BF), 'tensor', axis=0, tiled=True)  51.9 us
    psum x1, waiting for transfers between devices, shards(): gu_sum, down_sum = lax.psum((gu_part, down_part), 'dp')  43.1 us
    dot_general x32, matrix products, heads_dot(): return jnp.einsum(form, left, right, preferred_element_type=F32)  38.5 us
    dot_general x8, matrix products, mm_tn(): lax.dot_general(left, right, (((0,), (0,)), ((), ())), preferred_element_...  28.2 us
  transfers between devices with their start and end apart: 13, of which 11 were waited for; matrix products, arithmetic and copies ran while one was open for 20% of the time, Pallas kernels for 0%

profile of v1, /device:TPU:0, one launch (start us, length us, event | category | flops | bytes accessed | tf_op | source)
XLA Modules:
  0.0 781.7 jit_solution(5054771073759842629)
XLA Ops:
  20.6 5.5 concatenate.63
  36.2 7.5 fusion.322
  84.4 6.0 multiply_convert_fusion.14
  107.9 6.0 psum.63
  119.2 32.6 %reduce-scatter.6.cloned.1.call-done = bf16[256,1024]{1,0:T(8,128)(2,1)} async-done(((bf16[1024,1024]{1,0:T(8,128)(2,1)}), bf16[256,1024]{1,0:T(8,128)(2,1)}) %reduce-scatter.6.cloned.1.call-update) | async-done | bytes 524304 | tf_op jit(solution)/shard_map/reduce_scatter | solution.py:196
  156.9 6.0 fusion.310
  164.8 14.2 %all-gather.8.cloned.1.call-done = bf16[1024,1024]{1,0:T(8,128)(2,1)} async-done(((bf16[256,1024]{1,0:T(8,128)(2,1)}), bf16[1024,1024]{1,0:T(8,128)(2,1)}) %all-gather.8.cloned.1.call-update) | async-done | bytes 2097168 | tf_op jit(solution)/shard_map/all_gather | solution.py:192
  179.0 6.6 fusion.59
  185.5 17.5 %all-gather.10.cloned.1.call-done = bf16[1024,1024]{1,0:T(8,128)(2,1)} async-done(((bf16[256,1024]{1,0:T(8,128)(2,1)}), bf16[1024,1024]{1,0:T(8,128)(2,1)}) %all-gather.10.cloned.1.call-update) | async-done | bytes 2097168 | tf_op jit(solution)/shard_map/all_gather | solution.py:192
  203.1 6.1 fusion.30
  214.3 31.5 %reduce-scatter.8.cloned.1.call-done = bf16[256,1024]{1,0:T(8,128)(2,1)} async-done(((bf16[1024,1024]{1,0:T(8,128)(2,1)}), bf16[256,1024]{1,0:T(8,128)(2,1)}) %reduce-scatter.8.cloned.1.call-update) | async-done | bytes 524304 | tf_op jit(solution)/shard_map/reduce_scatter | solution.py:196
  252.1 5.9 convolution_convert_fusion
  258.0 16.6 %all-gather.12.cloned.1.call-done = bf16[1024,1024]{1,0:T(8,128)(2,1)} async-done(((bf16[256,1024]{1,0:T(8,128)(2,1)}), bf16[1024,1024]{1,0:T(8,128)(2,1)}) %all-gather.12.cloned.1.call-update) | async-done | bytes 2097168 | tf_op jit(solution)/shard_map/all_gather | solution.py:192
  299.1 6.1 psum.64
  355.6 8.7 %multiply_reduce_fusion.7 = (f32[384]{0:T(512)}, f32[384]{0:T(512)}, f32[384]{0:T(512)}, f32[384]{0:T(512)S(1)}, f32[384]{0:T(512)}, /*index=5*/f32[1024,384]{1,0:T(8,128)}, f32[1024,384]{1,0:T(8,128)}, f32[1024,384]{1,0:T(8,128)}) fusion(f32[1024,384]{1,0:T(8,128)} %split.43, f32[1024,1408]{1,0:T(8,128)} %copy-done.3, ...), kind=kLoop, calls=%fused_computation.91 | loop fusion | flops 11008128 | bytes 17310720 | tf_op jit(solution)/shard_map/transpose(jvp())/reduce_sum | solution.py:49
  394.7 43.1 %all-reduce.30.cloned.1.call-done = bf16[1024,1024]{1,0:T(8,128)(2,1)} async-done(((bf16[1024,1024]{1,0:T(8,128)(2,1)}), bf16[1024,1024]{1,0:T(8,128)(2,1)}) %all-reduce.30.cloned.1.call-update) | async-done | bytes 2097168 | tf_op jit(solution)/shard_map/psum | solution.py:320
  438.1 8.4 %fusion.338 = (bf16[1024,1408]{1,0:T(8,128)(2,1)S(1)}, f32[1024,1408]{1,0:T(8,128)}) fusion(bf16[1024,1024]{1,0:T(8,128)(2,1)} %all-gather.6.cloned.1.call-done, bf16[1024,1408]{1,0:T(8,128)(2,1)} %concatenate.79), kind=kOutput, calls=%fused_computation.520 | convolution fusion | flops 2954231808 | bytes 13631488 | tf_op jit(solution)/shard_map/dot_general | solution.py:24
  457.8 61.9 %all-reduce.32.cloned.1.call-done = bf16[512,1024]{1,0:T(8,128)(2,1)} async-done(((bf16[512,1024]{1,0:T(8,128)(2,1)}), bf16[512,1024]{1,0:T(8,128)(2,1)}) %all-reduce.32.cloned.1.call-update) | async-done | bytes 1048592 | tf_op jit(solution)/shard_map/psum | solution.py:325
  519.7 27.8 %reduce-scatter.14.cloned.1.call-done = bf16[256,512]{1,0:T(8,128)(2,1)} async-done(((bf16[1024,512]{1,0:T(8,128)(2,1)}), bf16[256,512]{1,0:T(8,128)(2,1)}) %reduce-scatter.14.cloned.1.call-update) | async-done | bytes 262160 | tf_op jit(solution)/shard_map/reduce_scatter | solution.py:375
  547.5 7.5 convolution_convert_fusion.1
  561.2 40.1 %psum.70 = f32[8466]{0:T(1024)S(1)} all-reduce(f32[8466]{0:T(1024)S(1)} %concatenate.82), channel_id=1, replica_groups=mesh['dp'=8,'tensor'=4] {'dp'}, use_global_device_ids=true, to_apply=%region_51.52 | all-reduce | flops 8466 | bytes 67728 | tf_op jit(solution)/shard_map/psum | solution.py:395
  614.4 68.5 %all-reduce.34.cloned.1.call-done = (bf16[1024,896]{1,0:T(8,128)(2,1)}, bf16[256,512]{1,0:T(8,128)(2,1)}, bf16[512,1024]{1,0:T(8,128)(2,1)}) async-done(((bf16[1024,896]{1,0:T(8,128)(2,1)}, bf16[256,512]{1,0:T(8,128)(2,1)}, bf16[512,1024]{1,0:T(8,128)(2,1)}), (bf16[1024,896]{1,0:T(8,128)(2,1)}, bf16[256,512]{1,0:T(8,128)(2,1)}, bf16[512,1024]{1,0:T(8,128)(2,1)})) %all-reduce.34.cloned.1.call-update) | async-done | bytes 3145744 | tf_op jit(solution)/shard_map/psum | solution.py:376
  682.9 33.7 %reduce-scatter.12.cloned.1.call-done = bf16[256,1024]{1,0:T(8,128)(2,1)} async-done(((bf16[1024,1024]{1,0:T(8,128)(2,1)}), bf16[256,1024]{1,0:T(8,128)(2,1)}) %reduce-scatter.12.cloned.1.call-update) | async-done | bytes 524304 | tf_op jit(solution)/shard_map/reduce_scatter | solution.py:196
  718.1 39.7 %psum.65 = f32[3328]{0:T(1024)S(1)} all-reduce(f32[3328]{0:T(1024)S(1)} %pad_maximum_fusion.18), channel_id=1, replica_groups=mesh['dp'=8,'tensor'=4] {'dp','tensor'}, use_global_device_ids=true, to_apply=%region_35.36 | all-reduce | flops 3328 | bytes 26624 | tf_op jit(solution)/shard_map/psum | solution.py:395
  (557 shorter events, 257.3 us)
Async XLA Ops:
  7.2 195.9 %copy-start = (bf16[512,1024]{1,0:T(8,128)(2,1)S(1)}, bf16[512,1024]{1,0:T(8,128)(2,1)}, u32[]{:S(2)}) copy-start(bf16[512,1024]{1,0:T(8,128)(2,1)} %param.43) | copy-start | bytes 3145732
  7.2 28.9 %all-gather.6.cloned.1.call-start = ((), (), s32[]{:S(2)}) async-start(), calls=%async_computation.5 | async-start | bytes 2621440 | tf_op jit(solution)/shard_map/all_gather | solution.py:192
  10.7 141.0 %reduce-scatter.6.cloned.1.call-start = ((), (), s32[]{:S(2)}) async-start(), calls=%async_computation.6 | async-start | bytes 2621440 | tf_op jit(solution)/shard_map/reduce_scatter | solution.py:196
  119.1 59.8 %all-gather.8.cloned.1.call-start = ((), (), s32[]{:S(2)}) async-start(), calls=%async_computation.7 | async-start | bytes 2621440 | tf_op jit(solution)/shard_map/all_gather | solution.py:192
  156.2 46.8 %all-gather.10.cloned.1.call-start = ((), (), s32[]{:S(2)}) async-start(), calls=%async_computation.8 | async-start | bytes 2621440 | tf_op jit(solution)/shard_map/all_gather | solution.py:192
  156.8 89.0 %reduce-scatter.8.cloned.1.call-start = ((), (), s32[]{:S(2)}) async-start(), calls=%async_computation.9 | async-start | bytes 2621440 | tf_op jit(solution)/shard_map/reduce_scatter | solution.py:196
  214.3 60.4 %all-gather.12.cloned.1.call-start = ((), (), s32[]{:S(2)}) async-start(), calls=%async_computation.10 | async-start | bytes 2621440 | tf_op jit(solution)/shard_map/all_gather | solution.py:192
  251.9 185.9 %all-reduce.30.cloned.1.call-start = ((), (), s32[]{:S(2)}) async-start(), calls=%async_computation.13 | async-start | bytes 4194304 | tf_op jit(solution)/shard_map/psum | solution.py:320
  334.7 185.0 %all-reduce.32.cloned.1.call-start = ((), (), s32[]{:S(2)}) async-start(), calls=%async_computation.14 | async-start | bytes 2097152 | tf_op jit(solution)/shard_map/psum | solution.py:325
  437.9 109.6 %reduce-scatter.14.cloned.1.call-start = ((), (), s32[]{:S(2)}) async-start(), calls=%async_computation.15 | async-start | bytes 1310720 | tf_op jit(solution)/shard_map/reduce_scatter | solution.py:375
  451.9 231.0 %all-reduce.34.cloned.1.call-start = ((), (), s32[]{:S(2)}) async-start(), calls=%async_computation.17 | async-start | bytes 6291456 | tf_op jit(solution)/shard_map/psum | solution.py:376
  547.5 169.1 %reduce-scatter.12.cloned.1.call-start = ((), (), s32[]{:S(2)}) async-start(), calls=%async_computation.12 | async-start | bytes 2621440 | tf_op jit(solution)/shard_map/reduce_scatter | solution.py:196
  555.0 204.6 %reduce-scatter.10.cloned.1.call-start = ((), (), s32[]{:S(2)}) async-start(), calls=%async_computation.11 | async-start | bytes 2621440 | tf_op jit(solution)/shard_map/reduce_scatter | solution.py:196
  559.0 211.4 %all-gather.14.cloned.1.call-start = ((), (), s32[]{:S(2)}) async-start(), calls=%async_computation.16 | async-start | bytes 1310720 | tf_op jit(solution)/shard_map/all_gather | solution.py:377
  612.2 104.4 %copy-start.78 = (f32[1024]{0:T(1024)S(1)}, f32[1024]{0:T(1024)}, u32[]{:S(2)}) copy-start(f32[1024]{0:T(1024)} %param.25) | copy-start | bytes 12292
  612.2 104.4 %copy-start.98 = (f32[256]{0:T(256)S(1)}, f32[256]{0:T(256)}, u32[]{:S(2)}) copy-start(f32[256]{0:T(256)} %copy-done.97) | copy-start | bytes 3076
  613.0 105.1 %copy-start.93 = (f32[1024]{0:T(1024)S(1)}, f32[1024]{0:T(1024)}, u32[]{:S(2)}) copy-start(f32[1024]{0:T(1024)} %get-tuple-element.167) | copy-start | bytes 12292
  613.0 105.1 %copy-start.132 = (f32[256]{0:T(256)S(1)}, f32[256]{0:T(256)}, u32[]{:S(2)}) copy-start(f32[256]{0:T(256)} %get-tuple-element.172) | copy-start | bytes 3076
  613.0 146.6 %copy-start.110 = (f32[256]{0:T(256)S(1)}, f32[256]{0:T(256)}, u32[]{:S(2)}) copy-start(f32[256]{0:T(256)} %copy-done.109) | copy-start | bytes 3076
  613.0 146.6 %copy-start.7 = (bf16[256,1024]{1,0:T(8,128)(2,1)S(1)}, bf16[256,1024]{1,0:T(8,128)(2,1)}, u32[]{:S(2)}) copy-start(bf16[256,1024]{1,0:T(8,128)(2,1)} %reduce-scatter.6.cloned.1.call-done) | copy-start | bytes 1572868
  613.0 146.7 %copy-start.19 = (bf16[256,1024]{1,0:T(8,128)(2,1)S(1)}, bf16[256,1024]{1,0:T(8,128)(2,1)}, u32[]{:S(2)}) copy-start(bf16[256,1024]{1,0:T(8,128)(2,1)} %param.23) | copy-start | bytes 1572868
  613.0 146.7 %copy-start.20 = (bf16[256,1024]{1,0:T(8,128)(2,1)S(1)}, bf16[256,1024]{1,0:T(8,128)(2,1)}, u32[]{:S(2)}) copy-start(bf16[256,1024]{1,0:T(8,128)(2,1)} %reduce-scatter.8.cloned.1.call-done) | copy-start | bytes 1572868
  613.0 146.7 %copy-start.80 = (f32[256]{0:T(256)S(1)}, f32[256]{0:T(256)}, u32[]{:S(2)}) copy-start(f32[256]{0:T(256)} %copy-done.79) | copy-start | bytes 3076
  613.1 146.7 %copy-start.100 = (f32[256]{0:T(256)S(1)}, f32[256]{0:T(256)}, u32[]{:S(2)}) copy-start(f32[256]{0:T(256)} %copy-done.99) | copy-start | bytes 3076
  (141 other events, 1091.6 us)
Sparse Core Ops, SparseCore 0:
  10.9 25.2 all-gather.5
  119.3 32.4 reduce-scatter.5
  156.4 22.5 all-gather.7
  180.5 22.5 all-gather.9
  214.4 31.4 reduce-scatter.7
  252.0 22.5 all-gather.11
  334.8 102.9 all-reduce.29
  441.9 77.7 all-reduce.31
  522.9 24.5 reduce-scatter.13
  551.8 131.0 all-reduce.33
  686.2 30.3 reduce-scatter.11
  719.6 31.5 reduce-scatter.9
  752.8 16.7 all-gather.13
